TPU v7x, 32 devices: a whole 2x2x4 slice. The times are simulated.
32 devices in a mesh: dp: 4 (over z), mp: 8 (over y, x, core).
Axes of the slice: x: 2, y: 2, z: 4, core: 2. Of those that a mesh axis runs over, the one named last changes fastest.
Arguments:
- node_feats: bfloat16 [65536, 128], P(('dp', 'mp')), may hold values from -6 to 6
- batch_deg: int32 [65536], P(('dp', 'mp')), may hold values from 1 to 8
- batch_nbrs: int32 [65536, 8], P(('dp', 'mp')), may hold values from 0 to 2047
- halo_nbrs: int32 [65536, 8], P(('dp', 'mp')), may hold values from 0 to 511
- halo_len: int32 [65536], P(('dp', 'mp')), may hold values from 1 to 8
- halo_rows: int32 [16384], P(('dp', 'mp')), may hold values from 0 to 65535, as said below
- halo_deg: int32 [16384], P(('dp', 'mp')), may hold values from 1 to 8
- feat_table: bfloat16 [65536, 128], P(('dp', 'mp')), may hold values from -6 to 6
- emb_table: bfloat16 [65536, 512], P(('dp', 'mp')), may hold values from -4 to 4
- grad_table: bfloat16 [65536, 512], P(('dp', 'mp')), may hold values from -6 to 6
- weight_one: bfloat16 [128, 512], replicated, may hold values from -0.5 to 0.5
- weight_two: bfloat16 [512, 512], replicated, may hold values from -0.25 to 0.25
- grad_out: bfloat16 [65536, 512], P(('dp', 'mp')), may hold values from -6 to 6
Outputs:
- out_embed: bfloat16 [65536, 512], P(('dp', 'mp'))
- halo_grad: bfloat16 [65536, 512], P(('dp', 'mp'))
- grad_one: float32 [128, 512], replicated
- grad_two: float32 [512, 512], replicated
Inputs may be any that keep to these rules, and one draw needn't show every extreme that they name: `halo_rows`: slot s of each device's 512 halo slots names a row of the block of 2048 rows held by device s // 16 of dp+mp (device index dp * 8 + mp), so that every device asks every owner for exactly 16 rows; rows may repeat.
All inputs are finite; a program needn't handle non-finite values.
Results may differ from a plain program's by a relative error of at most 0.006.
Values may be sent and summed in bfloat16 or wider, within the bound.
A program may use at most 128 MiB of HBM per device.

v0:
```python
import functools

import jax
import jax.numpy as jnp
from jax import lax
from jax.experimental import pallas as pl
from jax.experimental.pallas import tpu as pltpu
from jax.sharding import PartitionSpec as P

F32 = jnp.float32
BF16 = jnp.bfloat16
I32 = jnp.int32
LANES = 128
CHUNK = 256
NN = (((1,), (0,)), ((), ()))
NT = (((1,), (1,)), ((), ()))
TN = (((0,), (0,)), ((), ()))


def dot(left, right, dims=NN):
    return lax.dot_general(left, right, dims, preferred_element_type=F32)


def kernel(
    size_dp,
    size_mp,
    per_peer,
    factor,
    packed_hbm,
    feats_hbm,
    feat_hbm,
    emb_hbm,
    gradt_hbm,
    w1_hbm,
    w2_hbm,
    up_hbm,
    out_hbm,
    hgrad_hbm,
    g1_ref,
    g2_ref,
    packed,
    feats,
    feat_tab,
    emb_tab,
    grad_tab,
    w1,
    w2,
    up,
    ask_src,
    ask_mid,
    ask_turn,
    ask_fin,
    inv_col,
    hinv_col,
    adj_t,
    hal_t,
    sel,
    x_src,
    x_mid,
    x_fin,
    e_src,
    e_mid,
    e_fin,
    v_src,
    v_mid,
    v_fin,
    p_src,
    p_mid,
    p_fin,
    feats_t,
    agg1_t,
    hid_t,
    dfac_t,
    own2_t,
    agg2_t,
    spread_own,
    term1,
    term2,
    out_buf,
    hgrad_buf,
    t1_src,
    t1_mid,
    t1_sum,
    t1_fin,
    t1_all,
    t2_src,
    t2_mid,
    t2_sum,
    t2_fin,
    t2_all,
    load_sem,
    store_sem,
    self_sem,
    send_mp,
    recv_mp,
    send_dp,
    recv_dp,
):
    me_dp = lax.axis_index("dp")
    me_mp = lax.axis_index("mp")
    rows = adj_t.shape[0]
    halo = hal_t.shape[0]
    group = size_mp * per_peer

    def load(at, source, target):
        return pltpu.make_async_copy(source, target, load_sem.at[at])

    loads = {
        "packed": load(0, packed_hbm, packed),
        "emb": load(1, emb_hbm, emb_tab),
        "feat": load(2, feat_hbm, feat_tab),
        "gradt": load(3, gradt_hbm, grad_tab),
        "up": load(4, up_hbm, up),
        "feats": load(5, feats_hbm, feats),
        "w1": load(6, w1_hbm, w1),
        "w2": load(7, w2_hbm, w2),
    }
    for name in ("packed", "feat", "emb", "gradt", "up", "feats", "w1", "w2"):
        loads[name].start()

    peers_mp = [lax.rem(me_mp + step, size_mp) for step in range(1, size_mp)]
    peers_dp = [lax.rem(me_dp + step, size_dp) for step in range(1, size_dp)]
    barrier = pltpu.get_barrier_semaphore()
    for peer in peers_mp:
        pl.semaphore_signal(barrier, inc=1, device_id=(me_dp, peer), device_id_type=pl.DeviceIdType.MESH)
    for peer in peers_dp:
        pl.semaphore_signal(barrier, inc=1, device_id=(peer, me_mp), device_id_type=pl.DeviceIdType.MESH)
    pl.semaphore_wait(barrier, size_mp - 1 + size_dp - 1)

    def to_mp(piece, peer, place, source, target):
        return pltpu.make_async_remote_copy(
            src_ref=source,
            dst_ref=target,
            send_sem=send_mp.at[piece, peer],
            recv_sem=recv_mp.at[piece, place],
            device_id=(me_dp, peer),
            device_id_type=pl.DeviceIdType.MESH,
        )

    def to_dp(piece, peer, place, source, target):
        return pltpu.make_async_remote_copy(
            src_ref=source,
            dst_ref=target,
            send_sem=send_dp.at[piece, peer],
            recv_sem=recv_dp.at[piece, place],
            device_id=(peer, me_mp),
            device_id_type=pl.DeviceIdType.MESH,
        )

    class Hop:
        def __init__(self, make, piece, me, peers, source_at, target_at, at):
            self.own = lambda: pltpu.make_async_copy(source_at(me), target_at(me), self_sem.at[at])
            self.out = [make(piece, peer, me, source_at(peer), target_at(me)) for peer in peers]
            self.come = [make(piece, peer, peer, source_at(peer), target_at(peer)) for peer in peers]

        def start(self):
            for copy in self.out:
                copy.start()
            self.own().start()

        def arrive(self):
            self.own().wait()
            for copy in self.come:
                copy.wait_recv()

        def finish(self):
            for copy in self.out:
                copy.wait_send()

    def block(ref, peer):
        return ref.at[:, pl.ds(pl.multiple_of(peer * per_peer, per_peer), per_peer), :]

    hops = []

    def hop_mp(piece, source_at, target_at):
        hop = Hop(to_mp, piece, me_mp, peers_mp, source_at, target_at, len(hops))
        hops.append(hop)
        return hop

    def hop_dp(piece, source_at, target_at):
        hop = Hop(to_dp, piece, me_dp, peers_dp, source_at, target_at, len(hops))
        hops.append(hop)
        return hop

    def swap(piece, source, middle, final):
        first = hop_mp(piece, lambda peer: block(source, peer), lambda peer: block(middle, peer))
        second = hop_dp(piece, lambda peer: middle.at[peer], lambda peer: final.at[peer])
        return first, second

    ask_one = hop_mp(0, lambda peer: ask_src, lambda peer: ask_mid.at[peer])
    ask_two = hop_dp(0, lambda peer: ask_turn.at[peer], lambda peer: ask_fin.at[peer])
    x_one, x_two = swap(1, x_src, x_mid, x_fin)
    e_one, e_two = swap(2, e_src, e_mid, e_fin)
    v_one, v_two = swap(3, v_src, v_mid, v_fin)
    p_one, p_two = swap(4, p_src, p_mid, p_fin)
    t2_one = hop_mp(5, lambda peer: t2_src.at[peer], lambda peer: t2_mid.at[peer])
    t2_two = hop_dp(5, lambda peer: t2_sum, lambda peer: t2_fin.at[peer])
    t1_one = hop_mp(6, lambda peer: t1_src.at[peer], lambda peer: t1_mid.at[peer])
    t1_two = hop_dp(6, lambda peer: t1_sum, lambda peer: t1_fin.at[peer])
    t2_three = hop_mp(7, lambda peer: t2_all.at[me_mp], lambda peer: t2_all.at[peer])
    t1_three = hop_mp(8, lambda peer: t1_all.at[me_mp], lambda peer: t1_all.at[peer])

    def gather_start(hop):
        for copy in hop.out:
            copy.start()

    def gather_arrive(hop):
        for copy in hop.come:
            copy.wait_recv()

    loads["packed"].wait()
    slots = batch_slots = 8
    line = 2 * batch_slots
    for part in range(size_dp):
        offsets = packed[line + 2 : line + 3, halo + part * group : halo + (part + 1) * group]
        ask_src[part * 8 : part * 8 + 8, :] = jnp.broadcast_to(offsets, (8, group))
    ask_one.start()

    inv_row = lax.rsqrt(packed[line : line + 1, :].astype(F32))
    hinv_row = lax.rsqrt(packed[line + 2 : line + 3, 0:halo].astype(F32))
    for at in range(rows // LANES):
        piece = inv_row[:, at * LANES : (at + 1) * LANES]
        inv_col[at * LANES : (at + 1) * LANES, :] = jnp.broadcast_to(piece, (LANES, LANES)).T
    for at in range(halo // LANES):
        piece = hinv_row[:, at * LANES : (at + 1) * LANES]
        hinv_col[at * LANES : (at + 1) * LANES, :] = jnp.broadcast_to(piece, (LANES, LANES)).T

    def fill(target, column, words_rows, first, extra, scale_col, lanes):
        row_at = lax.broadcasted_iota(I32, (words_rows, LANES), 0)
        words = jnp.zeros((words_rows, LANES), I32)
        shift_by = words_rows.bit_length() - 1
        picks = []
        for slot in range(slots):
            index = packed[first + slot : first + slot + 1, lanes]
            value = lax.shift_left(jnp.ones_like(index), 4 * lax.shift_right_logical(index, shift_by))
            if extra is None:
                length = packed[line + 1 : line + 2, lanes]
                value = jnp.where(length > slot, value, 0)
            picks.append((index, value))
        if extra is not None:
            value = lax.shift_left(jnp.ones_like(extra), 4 * lax.shift_right_logical(extra, shift_by))
            picks.append((extra, value))
        for index, value in picks:
            low = jnp.bitwise_and(index, words_rows - 1)
            words = words + jnp.where(low == row_at, value, 0)
        inv_here = lax.rsqrt(packed[line : line + 1, lanes].astype(F32))
        for nibble in range(8):
            count = jnp.bitwise_and(lax.shift_right_logical(words, 4 * nibble), 15)
            span = slice(nibble * words_rows, (nibble + 1) * words_rows)
            tile = count.astype(F32) * (scale_col[span, :] * inv_here)
            target[span, lanes] = tile.astype(BF16)

    def fill_halo(column, carry):
        lanes = pl.ds(pl.multiple_of(column * LANES, LANES), LANES)
        fill(hal_t, column, halo // 8, batch_slots, None, hinv_col, lanes)
        return carry

    def fill_adj(column, carry):
        lanes = pl.ds(pl.multiple_of(column * LANES, LANES), LANES)
        own = lax.broadcasted_iota(I32, (1, LANES), 1) + column * LANES
        fill(adj_t, column, rows // 8, 0, own, inv_col, lanes)
        return carry

    columns = rows // LANES
    lax.fori_loop(0, columns, fill_halo, 0)

    ask_one.arrive()
    lane_group = lax.broadcasted_iota(I32, (size_dp * 8, group), 1) // per_peer
    turned = jnp.zeros((size_dp * 8, group), I32)
    for source in range(size_mp):
        shift = lax.rem(source - me_mp + size_mp, size_mp) * per_peer
        moved = pltpu.roll(ask_mid[source], shift, 1)
        turned = jnp.where(lane_group == source, moved, turned)
    for part in range(size_dp):
        ask_turn[part] = turned[part * 8 : part * 8 + 8, :]
    ask_two.start()

    lax.fori_loop(0, columns // 4, fill_adj, 0)

    ask_two.arrive()
    lane_at = lax.broadcasted_iota(I32, (group, LANES), 1)
    for part in range(size_dp):
        ask_col = jnp.broadcast_to(ask_fin[part, 0:1, :], (LANES, group)).T

        def fill_sel(column, carry, ask_col=ask_col, part=part):
            lanes = pl.ds(pl.multiple_of(column * LANES, LANES), LANES)
            hit = ask_col == lane_at + column * LANES
            sel[part * group : (part + 1) * group, lanes] = jnp.where(hit, 1.0, 0.0).astype(BF16)
            return carry

        lax.fori_loop(0, columns, fill_sel, 0)

    def pick(table, target):
        def body(part, carry):
            here = pl.ds(pl.multiple_of(part * group, group), group)
            target[part] = dot(sel[here, :], table[...]).astype(BF16)
            return carry

        lax.fori_loop(0, size_dp, body, 0)

    loads["feat"].wait()
    pick(feat_tab, x_src)
    x_one.start()
    loads["emb"].wait()
    pick(emb_tab, e_src)
    e_one.start()
    loads["gradt"].wait()
    pick(grad_tab, v_src)
    v_one.start()

    lax.fori_loop(columns // 4, columns, fill_adj, 0)

    x_one.arrive()
    x_two.start()

    chunks = rows // CHUNK

    def at_chunk(step):
        return pl.ds(pl.multiple_of(step * CHUNK, CHUNK), CHUNK)

    loads["up"].wait()
    for part in range(size_dp):
        p_src[part] = dot(hal_t[part * group : (part + 1) * group, :], up[...]).astype(BF16)

    e_one.arrive()
    e_two.start()

    def own_spread(step, carry):
        here = at_chunk(step)
        spread_own[here, :] = dot(adj_t[here, :], up[...])
        return carry

    lax.fori_loop(0, chunks // 2, own_spread, 0)
    v_one.arrive()
    v_two.start()
    p_one.start()
    lax.fori_loop(chunks // 2, chunks, own_spread, 0)

    loads["feats"].wait()
    feats_t[...] = feats[...].T
    loads["w1"].wait()
    w1_t = w1[...].T
    x_two.arrive()
    hx_t = x_fin[...].reshape(halo, x_fin.shape[-1]).T

    def layer_one(step, carry):
        here = at_chunk(step)
        agg = (dot(feats_t[...], adj_t[:, here]) + dot(hx_t, hal_t[:, here])).astype(BF16)
        agg1_t[:, here] = agg
        pre = dot(w1_t, agg)
        sigma = jax.nn.sigmoid(pre)
        hid_t[:, here] = (pre * sigma).astype(BF16)
        dfac_t[:, here] = sigma * (1.0 + pre * (1.0 - sigma))
        return carry

    lax.fori_loop(0, chunks, layer_one, 0)

    def own_two(step, carry):
        here = at_chunk(step)
        own2_t[:, here] = dot(hid_t[...], adj_t[:, here])
        return carry

    lax.fori_loop(0, chunks, own_two, 0)

    p_one.arrive()
    p_two.start()

    e_two.arrive()
    he_t = e_fin[...].reshape(halo, e_fin.shape[-1]).T

    def layer_two(step, carry):
        here = at_chunk(step)
        agg2_t[:, here] = (own2_t[:, here] + dot(he_t, hal_t[:, here])).astype(BF16)
        return carry

    lax.fori_loop(0, chunks, layer_two, 0)
    part2 = t2_src.shape[1]
    for peer in range(size_mp):
        strip = agg2_t[peer * part2 : (peer + 1) * part2, :]
        t2_src[peer] = dot(strip, up[...]).astype(BF16)
    t2_one.start()

    loads["w2"].wait()
    v_two.arrive()
    term1[...] = jnp.zeros_like(term1)
    hv = v_fin[...].reshape(halo, v_fin.shape[-1])

    def backward(step, carry):
        here = at_chunk(step)
        spread = (spread_own[here, :] + dot(hal_t[:, here], hv, TN)).astype(BF16)
        back = dot(w2[...], spread, NT)
        d_pre = (back * dfac_t[:, here]).astype(BF16)
        term1[...] += dot(agg1_t[:, here], d_pre, NT)
        return carry

    lax.fori_loop(0, chunks, backward, 0)
    part1 = t1_src.shape[1]
    for peer in range(size_mp):
        t1_src[peer] = term1[peer * part1 : (peer + 1) * part1, :].astype(BF16)
    t1_one.start()

    def total(ref, count):
        value = ref[0].astype(F32)
        for at in range(1, count):
            value = value + ref[at].astype(F32)
        return value

    t2_one.arrive()
    t2_sum[...] = total(t2_mid, size_mp).astype(BF16)
    t2_two.start()

    def output(step, carry):
        here = at_chunk(step)
        out_buf[here, :] = dot(agg2_t[:, here], w2[...], TN).astype(BF16)
        return carry

    lax.fori_loop(0, chunks, output, 0)
    out_store = pltpu.make_async_copy(out_buf, out_hbm, store_sem.at[0])
    out_store.start()

    t1_one.arrive()
    t1_sum[...] = total(t1_mid, size_mp).astype(BF16)
    t1_two.start()
    t2_two.arrive()
    t2_all[me_mp] = (total(t2_fin, size_dp) * factor).astype(BF16)
    gather_start(t2_three)

    p_two.arrive()
    hp = p_fin[...].reshape(halo, p_fin.shape[-1])

    def owner_sum(step, carry):
        here = at_chunk(step)
        hgrad_buf[here, :] = dot(sel[:, here], hp, TN).astype(BF16)
        return carry

    lax.fori_loop(0, chunks // 2, owner_sum, 0)
    t1_two.arrive()
    t1_all[me_mp] = (total(t1_fin, size_dp) * factor).astype(BF16)
    gather_start(t1_three)
    lax.fori_loop(chunks // 2, chunks, owner_sum, 0)
    hgrad_store = pltpu.make_async_copy(hgrad_buf, hgrad_hbm, store_sem.at[1])
    hgrad_store.start()

    gather_arrive(t2_three)
    for peer in range(size_mp):
        g2_ref[peer * part2 : (peer + 1) * part2, :] = t2_all[peer].astype(F32)
    gather_arrive(t1_three)
    for peer in range(size_mp):
        g1_ref[peer * part1 : (peer + 1) * part1, :] = t1_all[peer].astype(F32)
    for hop in hops:
        hop.finish()
    out_store.wait()
    hgrad_store.wait()


def local_kernel(
    node_feats,
    batch_deg,
    batch_nbrs,
    halo_nbrs,
    halo_len,
    halo_rows,
    halo_deg,
    feat_table,
    emb_table,
    grad_table,
    weight_one,
    weight_two,
    grad_out,
):
    size_dp = lax.axis_size("dp")
    size_mp = lax.axis_size("mp")
    rows, feat = node_feats.shape
    halo = halo_rows.shape[0]
    shard_rows = feat_table.shape[0]
    hid_in, hid = weight_two.shape
    per_peer = halo // (size_dp * size_mp)
    group = size_mp * per_peer
    factor = 1.0 / float(rows * size_dp * size_mp) ** 0.5
    tail = jnp.concatenate([halo_deg, halo_rows % shard_rows, jnp.zeros((rows - 2 * halo,), I32)])
    packed = jnp.concatenate(
        [
            batch_nbrs.T,
            halo_nbrs.T,
            batch_deg[None],
            halo_len[None],
            tail[None],
            jnp.zeros((5, rows), I32),
        ]
    )
    any_spec = pl.BlockSpec(memory_space=pl.ANY)
    vmem_spec = pl.BlockSpec(memory_space=pltpu.VMEM)
    vmem = pltpu.VMEM
    part1, part2 = feat // size_mp, hid // size_mp

    def three(width):
        return [vmem((size_dp, group, width), BF16)] * 3

    def sums(part):
        return [
            vmem((size_mp, part, hid), BF16),
            vmem((size_mp, part, hid), BF16),
            vmem((part, hid), BF16),
            vmem((size_dp, part, hid), BF16),
            vmem((size_mp, part, hid), BF16),
        ]

    return pl.pallas_call(
        functools.partial(kernel, size_dp, size_mp, per_peer, factor),
        out_shape=(
            jax.ShapeDtypeStruct((rows, hid), BF16),
            jax.ShapeDtypeStruct((shard_rows, hid), BF16),
            jax.ShapeDtypeStruct((feat, hid), F32),
            jax.ShapeDtypeStruct((hid_in, hid), F32),
        ),
        in_specs=[any_spec] * 8,
        out_specs=(any_spec, any_spec, vmem_spec, vmem_spec),
        scratch_shapes=[
            vmem(packed.shape, I32),
            vmem(node_feats.shape, BF16),
            vmem(feat_table.shape, BF16),
            vmem(emb_table.shape, BF16),
            vmem(grad_table.shape, BF16),
            vmem(weight_one.shape, BF16),
            vmem(weight_two.shape, BF16),
            vmem(grad_out.shape, BF16),
            vmem((size_dp * 8, group), I32),
            vmem((size_mp, size_dp * 8, group), I32),
            vmem((size_dp, 8, group), I32),
            vmem((size_dp, 8, group), I32),
            vmem((rows, LANES), F32),
            vmem((halo, LANES), F32),
            vmem((rows, rows), BF16),
            vmem((halo, rows), BF16),
            vmem((halo, shard_rows), BF16),
            *three(feat),
            *three(hid),
            *three(hid),
            *three(hid),
            vmem((feat, rows), BF16),
            vmem((feat, rows), BF16),
            vmem((hid, rows), BF16),
            vmem((hid, rows), F32),
            vmem((hid, rows), F32),
            vmem((hid, rows), BF16),
            vmem((rows, hid), F32),
            vmem((feat, hid), F32),
            vmem((8, LANES), F32),
            vmem((rows, hid), BF16),
            vmem((shard_rows, hid), BF16),
            *sums(part1),
            *sums(part2),
            pltpu.SemaphoreType.DMA((8,)),
            pltpu.SemaphoreType.DMA((2,)),
            pltpu.SemaphoreType.DMA((16,)),
            pltpu.SemaphoreType.DMA((9, size_mp)),
            pltpu.SemaphoreType.DMA((9, size_mp)),
            pltpu.SemaphoreType.DMA((7, size_dp)),
            pltpu.SemaphoreType.DMA((7, size_dp)),
        ],
        compiler_params=pltpu.CompilerParams(
            collective_id=0, has_side_effects=True, vmem_limit_bytes=60 * 1024 * 1024
        ),
    )(packed, node_feats, feat_table, emb_table, grad_table, weight_one, weight_two, grad_out)


def matrices(batch_deg, batch_nbrs, halo_nbrs, halo_len, halo_deg):
    rows = batch_nbrs.shape[0]
    halo_count = halo_deg.shape[0]
    inv_batch = lax.rsqrt(batch_deg.astype(jnp.float32))
    inv_halo = lax.rsqrt(halo_deg.astype(jnp.float32))
    self_coef = 1.0 / batch_deg.astype(jnp.float32)
    row_index = jnp.arange(rows, dtype=jnp.int32)
    halo_index = jnp.arange(halo_count, dtype=jnp.int32)
    counts = jnp.zeros((rows, rows), jnp.float32)
    for slot in range(batch_nbrs.shape[1]):
        counts = counts + (batch_nbrs[:, slot, None] == row_index[None, :]).astype(jnp.float32)
    halo_counts = jnp.zeros((rows, halo_count), jnp.float32)
    for slot in range(halo_nbrs.shape[1]):
        hit = (halo_nbrs[:, slot, None] == halo_index[None, :]) & (halo_len[:, None] > slot)
        halo_counts = halo_counts + hit.astype(jnp.float32)
    diagonal = jnp.where(
        row_index[:, None] == row_index[None, :], self_coef[:, None], jnp.float32(0.0)
    )
    adjacency = (counts * (inv_batch[:, None] * inv_batch[None, :]) + diagonal).astype(jnp.bfloat16)
    halo_mat = (halo_counts * (inv_batch[:, None] * inv_halo[None, :])).astype(jnp.bfloat16)
    return (adjacency, halo_mat)


def mult(left, right):
    return jnp.dot(left, right, preferred_element_type=jnp.float32)


def mult_t(left, right):
    return lax.dot_general(
        left, right, (((0,), (0,)), ((), ())), preferred_element_type=jnp.float32
    )


def local_plain(
    node_feats,
    batch_deg,
    batch_nbrs,
    halo_nbrs,
    halo_len,
    halo_rows,
    halo_deg,
    feat_table,
    emb_table,
    grad_table,
    weight_one,
    weight_two,
    grad_out,
):
    batch_rows = node_feats.shape[0]
    hidden_width = weight_two.shape[1]
    feat_width = feat_table.shape[1]
    size_dp = lax.axis_size("dp")
    size_mp = lax.axis_size("mp")
    devices = size_dp * size_mp
    halo_count = halo_rows.shape[0]
    per_peer = halo_count // devices
    shard_rows = feat_table.shape[0]
    offsets = halo_rows % shard_rows
    asked = lax.all_to_all(
        offsets.reshape(devices, per_peer), ("dp", "mp"), split_axis=0, concat_axis=0, tiled=True
    )
    shard_index = jnp.arange(shard_rows, dtype=jnp.int32)
    selector = (asked.reshape(-1)[:, None] == shard_index[None, :]).astype(jnp.bfloat16)
    lead = asked.shape
    picked_x = mult(selector, feat_table).astype(jnp.bfloat16).reshape(lead + (feat_width,))
    picked_e = mult(selector, emb_table).astype(jnp.bfloat16).reshape(lead + (hidden_width,))
    picked_v = mult(selector, grad_table).astype(jnp.bfloat16).reshape(lead + (hidden_width,))
    pulled = (
        lax.all_to_all(picked_x, ("dp", "mp"), split_axis=0, concat_axis=0, tiled=True),
        lax.all_to_all(picked_e, ("dp", "mp"), split_axis=0, concat_axis=0, tiled=True),
        lax.all_to_all(picked_v, ("dp", "mp"), split_axis=0, concat_axis=0, tiled=True),
    )
    halo_x = pulled[0].reshape(halo_count, feat_width)
    halo_e = pulled[1].reshape(halo_count, hidden_width)
    halo_v = pulled[2].reshape(halo_count, hidden_width)
    adjacency, halo_mat = matrices(batch_deg, batch_nbrs, halo_nbrs, halo_len, halo_deg)
    agg_one = (mult(adjacency, node_feats) + mult(halo_mat, halo_x)).astype(jnp.bfloat16)
    pre_one = mult(agg_one, weight_one)
    hidden = jax.nn.silu(pre_one).astype(jnp.bfloat16)
    agg_two = (mult(adjacency, hidden) + mult(halo_mat, halo_e)).astype(jnp.bfloat16)
    out_embed = mult(agg_two, weight_two).astype(jnp.bfloat16)
    partial_value = mult_t(halo_mat, grad_out)
    arrived = lax.all_to_all(
        partial_value.reshape(devices, per_peer, hidden_width),
        ("dp", "mp"),
        split_axis=0,
        concat_axis=0,
        tiled=True,
    )
    halo_grad = lax.dot_general(
        selector.astype(jnp.float32),
        arrived.reshape(-1, hidden_width),
        (((0,), (0,)), ((), ())),
        precision=lax.Precision.HIGHEST,
        preferred_element_type=jnp.float32,
    )
    halo_grad = halo_grad.astype(jnp.bfloat16)
    spread = (mult_t(adjacency, grad_out) + mult(halo_mat, halo_v)).astype(jnp.bfloat16)
    back_hidden = lax.dot_general(
        spread, weight_two, (((1,), (1,)), ((), ())), preferred_element_type=jnp.float32
    )
    sigma = jax.nn.sigmoid(pre_one)
    d_pre = (back_hidden * (sigma * (1.0 + pre_one * (1.0 - sigma)))).astype(jnp.bfloat16)
    term_two = mult_t(agg_two, grad_out)
    term_one = mult_t(agg_one, d_pre)
    column_sums = (
        lax.psum_scatter(term_one, "mp", scatter_dimension=1, tiled=True),
        lax.psum_scatter(term_two, "mp", scatter_dimension=1, tiled=True),
    )
    column_sums = lax.psum((column_sums[0], column_sums[1]), "dp")
    summed = (
        lax.all_gather(column_sums[0], "mp", axis=1, tiled=True),
        lax.all_gather(column_sums[1], "mp", axis=1, tiled=True),
    )
    factor = 1.0 / jnp.sqrt(jnp.float32(batch_rows * devices))
    return (out_embed, halo_grad, summed[0] * factor, summed[1] * factor)


def local(*args):
    size_dp, size_mp = lax.axis_size("dp"), lax.axis_size("mp")
    rows, halo = args[0].shape[0], args[5].shape[0]
    per_peer = halo // (size_dp * size_mp)
    if per_peer % 16 == 0 and size_mp * per_peer == LANES and rows == args[7].shape[0]:
        return local_kernel(*args)
    return local_plain(*args)


def solution(mesh):
    return jax.shard_map(
        local,
        mesh=mesh,
        in_specs=(
            P(("dp", "mp"), None),
            P(("dp", "mp")),
            P(("dp", "mp"), None),
            P(("dp", "mp"), None),
            P(("dp", "mp")),
            P(("dp", "mp")),
            P(("dp", "mp")),
            P(("dp", "mp"), None),
            P(("dp", "mp"), None),
            P(("dp", "mp"), None),
            P(),
            P(),
            P(("dp", "mp"), None),
        ),
        out_specs=(P(("dp", "mp"), None), P(("dp", "mp"), None), P(), P()),
        check_vma=False,
    )
```

profile of v0, /device:TPU:0, one launch (start us, length us, event | category | flops | bytes accessed | tf_op | source)
XLA Modules:
  0.0 91.3 jit_solution(15875394645611624077)
XLA Ops:
  0.6 0.7 add_select_fusion
  1.3 0.7 pad_add_fusion
  2.0 4.3 %concatenate.7.packed_hbm = s32[24,2048]{1,0:T(8,128)} concatenate(s32[8,2048]{1,0:T(8,128)} %bitcast.5, s32[8,2048]{1,0:T(8,128)} %bitcast.6, s32[1,2048]{1,0:T(1,128)} %bitcast.8, s32[1,2048]{1,0:T(1,128)} %bitcast.9, s32[1,2048]{1,0:T(1,128)S(1)} %bitcast.7, s32[5,2048]{1,0:T(8,128)S(1)} %broadcast_in_dim.19), dimensions={0} | concatenate | bytes 393216 | tf_op jit(solution)/shard_map/concatenate | solution.py:481
  6.3 78.7 %shard_map.156 = (bf16[2048,512]{1,0:T(8,128)(2,1)}, bf16[2048,512]{1,0:T(8,128)(2,1)}, f32[128,512]{1,0:T(8,128)}, f32[512,512]{1,0:T(8,128)}) custom-call(s32[24,2048]{1,0:T(8,128)} %concatenate.7.packed_hbm, bf16[2048,128]{1,0:T(8,128)(2,1)} %feats_hbm.1, bf16[2048,128]{1,0:T(8,128)(2,1)} %feat_hbm.1, bf16[2048,512]{1,0:T(8,128)(2,1)} %emb_hbm.1, ...), custom_call_target="tpu_custom_call" | custom-call | tf_op jit(solution)/shard_map/pallas_call | solution.py:508
  85.1 0.0 copy-start
  85.1 3.2 %copy.21 = bf16[2048,512]{1,0:T(8,128)(2,1)} copy(bf16[2048,512]{1,0:T(8,128)(2,1)} %get-tuple-element.8) | data formatting | bytes 4194304
  88.3 0.0 copy-done
  88.3 0.0 copy-start.2
  88.3 0.0 copy-start.1
  88.3 1.3 %copy.22 = bf16[2048,512]{1,0:T(8,128)(2,1)} copy(bf16[2048,512]{1,0:T(8,128)(2,1)S(1)} %copy-done) | data formatting | bytes 4194304
  89.6 0.0 copy-done.2
  89.6 0.7 copy.23
  90.3 0.0 copy-done.1
  90.4 1.0 %copy.24 = f32[512,512]{1,0:T(8,128)} copy(f32[512,512]{1,0:T(8,128)S(1)} %copy-done.1) | data formatting | bytes 2097152
  (2 shorter events, 0.0 us)
Async XLA Ops:
  85.1 3.2 %copy-start = (bf16[2048,512]{1,0:T(8,128)(2,1)S(1)}, bf16[2048,512]{1,0:T(8,128)(2,1)}, u32[]{:S(2)}) copy-start(bf16[2048,512]{1,0:T(8,128)(2,1)} %get-tuple-element.9) | copy-start | bytes 6291460
  88.3 1.3 %copy-start.2 = (f32[128,512]{1,0:T(8,128)S(1)}, f32[128,512]{1,0:T(8,128)}, u32[]{:S(2)}) copy-start(f32[128,512]{1,0:T(8,128)} %get-tuple-element.10) | copy-start | bytes 786436
  88.3 2.1 %copy-start.1 = (f32[512,512]{1,0:T(8,128)S(1)}, f32[512,512]{1,0:T(8,128)}, u32[]{:S(2)}) copy-start(f32[512,512]{1,0:T(8,128)} %get-tuple-element.11) | copy-start | bytes 3145732
where the time goes:
time: 91.7 us; the launch traced here: 91.3 us
  Pallas kernels  78.7 us (86%)
  local copies, waits for them, and re-layouts  10.6 us (12%)
  other arithmetic  1.38 us (2%)
    pallas_call x1, Pallas kernels, local_kernel(): pl.pallas_call(functools.partial(kernel, size_dp, size_mp, per_peer, fact...  78.7 us
    unnamed x10, local copies, waits for them, and re-layouts  6.23 us
    concatenate x1, local copies, waits for them, and re-layouts, local_kernel(): jnp.concatenate([batch_nbrs.T, halo_nbrs.T, batch_deg[None], halo_len[Non...  4.33 us

commit v1 on v0

--- a/solution.py
+++ b/solution.py
@@ -12,6 +12,7 @@
 I32 = jnp.int32
 LANES = 128
 CHUNK = 256
+VMEM_MIB = 54
 NN = (((1,), (0,)), ((), ()))
 NT = (((1,), (1,)), ((), ()))
 TN = (((0,), (0,)), ((), ()))
@@ -26,7 +27,12 @@
     size_mp,
     per_peer,
     factor,
-    packed_hbm,
+    nbrs_hbm,
+    hnbrs_hbm,
+    deg_hbm,
+    len_hbm,
+    hdeg_hbm,
+    hrows_hbm,
     feats_hbm,
     feat_hbm,
     emb_hbm,
@@ -34,11 +40,16 @@
     w1_hbm,
     w2_hbm,
     up_hbm,
-    out_hbm,
-    hgrad_hbm,
+    out_buf,
+    hgrad_buf,
     g1_ref,
     g2_ref,
-    packed,
+    nbrs,
+    hnbrs,
+    deg,
+    length,
+    hdeg,
+    hrows,
     feats,
     feat_tab,
     emb_tab,
@@ -50,6 +61,7 @@
     ask_mid,
     ask_turn,
     ask_fin,
+    ask_col_ref,
     inv_col,
     hinv_col,
     adj_t,
@@ -67,6 +79,9 @@
     p_src,
     p_mid,
     p_fin,
+    q_src,
+    q_mid,
+    q_fin,
     feats_t,
     agg1_t,
     hid_t,
@@ -75,9 +90,7 @@
     agg2_t,
     spread_own,
     term1,
-    term2,
-    out_buf,
-    hgrad_buf,
+    hal,
     t1_src,
     t1_mid,
     t1_sum,
@@ -89,7 +102,6 @@
     t2_fin,
     t2_all,
     load_sem,
-    store_sem,
     self_sem,
     send_mp,
     recv_mp,
@@ -101,12 +113,18 @@
     rows = adj_t.shape[0]
     halo = hal_t.shape[0]
     group = size_mp * per_peer
+    shard_rows = sel.shape[1]
 
     def load(at, source, target):
         return pltpu.make_async_copy(source, target, load_sem.at[at])
 
     loads = {
-        "packed": load(0, packed_hbm, packed),
+        "hrows": load(0, hrows_hbm, hrows),
+        "nbrs": load(8, nbrs_hbm, nbrs),
+        "hnbrs": load(9, hnbrs_hbm, hnbrs),
+        "deg": load(10, deg_hbm, deg),
+        "length": load(11, len_hbm, length),
+        "hdeg": load(12, hdeg_hbm, hdeg),
         "emb": load(1, emb_hbm, emb_tab),
         "feat": load(2, feat_hbm, feat_tab),
         "gradt": load(3, gradt_hbm, grad_tab),
@@ -115,7 +133,9 @@
         "w1": load(6, w1_hbm, w1),
         "w2": load(7, w2_hbm, w2),
     }
-    for name in ("packed", "feat", "emb", "gradt", "up", "feats", "w1", "w2"):
+    for name in ("hrows", "deg", "hdeg", "length", "hnbrs", "nbrs", "up"):
+        loads[name].start()
+    for name in ("feat", "emb", "gradt", "feats", "w1", "w2"):
         loads[name].start()
 
     peers_mp = [lax.rem(me_mp + step, size_mp) for step in range(1, size_mp)]
@@ -193,12 +213,13 @@
     e_one, e_two = swap(2, e_src, e_mid, e_fin)
     v_one, v_two = swap(3, v_src, v_mid, v_fin)
     p_one, p_two = swap(4, p_src, p_mid, p_fin)
+    q_one, q_two = swap(7, q_src, q_mid, q_fin)
     t2_one = hop_mp(5, lambda peer: t2_src.at[peer], lambda peer: t2_mid.at[peer])
     t2_two = hop_dp(5, lambda peer: t2_sum, lambda peer: t2_fin.at[peer])
     t1_one = hop_mp(6, lambda peer: t1_src.at[peer], lambda peer: t1_mid.at[peer])
     t1_two = hop_dp(6, lambda peer: t1_sum, lambda peer: t1_fin.at[peer])
-    t2_three = hop_mp(7, lambda peer: t2_all.at[me_mp], lambda peer: t2_all.at[peer])
-    t1_three = hop_mp(8, lambda peer: t1_all.at[me_mp], lambda peer: t1_all.at[peer])
+    t2_three = hop_mp(8, lambda peer: t2_all.at[me_mp], lambda peer: t2_all.at[peer])
+    t1_three = hop_mp(9, lambda peer: t1_all.at[me_mp], lambda peer: t1_all.at[peer])
 
     def gather_start(hop):
         for copy in hop.out:
@@ -208,34 +229,32 @@
         for copy in hop.come:
             copy.wait_recv()
 
-    loads["packed"].wait()
-    slots = batch_slots = 8
-    line = 2 * batch_slots
+    loads["hrows"].wait()
     for part in range(size_dp):
-        offsets = packed[line + 2 : line + 3, halo + part * group : halo + (part + 1) * group]
+        offsets = lax.rem(hrows[part : part + 1, :], shard_rows)
         ask_src[part * 8 : part * 8 + 8, :] = jnp.broadcast_to(offsets, (8, group))
     ask_one.start()
 
-    inv_row = lax.rsqrt(packed[line : line + 1, :].astype(F32))
-    hinv_row = lax.rsqrt(packed[line + 2 : line + 3, 0:halo].astype(F32))
-    for at in range(rows // LANES):
-        piece = inv_row[:, at * LANES : (at + 1) * LANES]
-        inv_col[at * LANES : (at + 1) * LANES, :] = jnp.broadcast_to(piece, (LANES, LANES)).T
-    for at in range(halo // LANES):
-        piece = hinv_row[:, at * LANES : (at + 1) * LANES]
-        hinv_col[at * LANES : (at + 1) * LANES, :] = jnp.broadcast_to(piece, (LANES, LANES)).T
-
-    def fill(target, column, words_rows, first, extra, scale_col, lanes):
+    for name in ("deg", "hdeg", "length", "hnbrs"):
+        loads[name].wait()
+
+    def spread_out(target, source):
+        for at in range(source.shape[0]):
+            piece = lax.rsqrt(source[at : at + 1, :].astype(F32))
+            target[at * LANES : (at + 1) * LANES, :] = jnp.broadcast_to(piece, (LANES, LANES)).T
+
+    spread_out(hinv_col, hdeg)
+
+    def fill(target, column, words_rows, indices, extra, scale_col, lanes):
         row_at = lax.broadcasted_iota(I32, (words_rows, LANES), 0)
         words = jnp.zeros((words_rows, LANES), I32)
         shift_by = words_rows.bit_length() - 1
         picks = []
-        for slot in range(slots):
-            index = packed[first + slot : first + slot + 1, lanes]
+        for slot in range(indices.shape[0]):
+            index = indices[slot : slot + 1, lanes]
             value = lax.shift_left(jnp.ones_like(index), 4 * lax.shift_right_logical(index, shift_by))
             if extra is None:
-                length = packed[line + 1 : line + 2, lanes]
-                value = jnp.where(length > slot, value, 0)
+                value = jnp.where(length[pl.ds(column, 1), :] > slot, value, 0)
             picks.append((index, value))
         if extra is not None:
             value = lax.shift_left(jnp.ones_like(extra), 4 * lax.shift_right_logical(extra, shift_by))
@@ -243,7 +262,7 @@
         for index, value in picks:
             low = jnp.bitwise_and(index, words_rows - 1)
             words = words + jnp.where(low == row_at, value, 0)
-        inv_here = lax.rsqrt(packed[line : line + 1, lanes].astype(F32))
+        inv_here = lax.rsqrt(deg[pl.ds(column, 1), :].astype(F32))
         for nibble in range(8):
             count = jnp.bitwise_and(lax.shift_right_logical(words, 4 * nibble), 15)
             span = slice(nibble * words_rows, (nibble + 1) * words_rows)
@@ -252,13 +271,13 @@
 
     def fill_halo(column, carry):
         lanes = pl.ds(pl.multiple_of(column * LANES, LANES), LANES)
-        fill(hal_t, column, halo // 8, batch_slots, None, hinv_col, lanes)
+        fill(hal_t, column, halo // 8, hnbrs, None, hinv_col, lanes)
         return carry
 
     def fill_adj(column, carry):
         lanes = pl.ds(pl.multiple_of(column * LANES, LANES), LANES)
         own = lax.broadcasted_iota(I32, (1, LANES), 1) + column * LANES
-        fill(adj_t, column, rows // 8, 0, own, inv_col, lanes)
+        fill(adj_t, column, rows // 8, nbrs, own, inv_col, lanes)
         return carry
 
     columns = rows // LANES
@@ -275,20 +294,31 @@
         ask_turn[part] = turned[part * 8 : part * 8 + 8, :]
     ask_two.start()
 
-    lax.fori_loop(0, columns // 4, fill_adj, 0)
+    loads["up"].wait()
+    half = p_src.shape[2]
+    for part in range(size_dp):
+        message = dot(hal_t[part * group : (part + 1) * group, :], up[...]).astype(BF16)
+        p_src[part] = message[:, 0:half]
+        q_src[part] = message[:, half:]
+    p_one.start()
+    loads["nbrs"].wait()
+    spread_out(inv_col, deg)
 
     ask_two.arrive()
     lane_at = lax.broadcasted_iota(I32, (group, LANES), 1)
+    ask_cols = [jnp.broadcast_to(ask_fin[part, 0:1, :], (LANES, group)).T for part in range(size_dp)]
     for part in range(size_dp):
-        ask_col = jnp.broadcast_to(ask_fin[part, 0:1, :], (LANES, group)).T
-
-        def fill_sel(column, carry, ask_col=ask_col, part=part):
-            lanes = pl.ds(pl.multiple_of(column * LANES, LANES), LANES)
-            hit = ask_col == lane_at + column * LANES
-            sel[part * group : (part + 1) * group, lanes] = jnp.where(hit, 1.0, 0.0).astype(BF16)
-            return carry
-
-        lax.fori_loop(0, columns, fill_sel, 0)
+        ask_col_ref[part * group : (part + 1) * group, :] = ask_cols[part]
+
+    def fill_sel(column, carry):
+        lanes = pl.ds(pl.multiple_of(column * LANES, LANES), LANES)
+        here = lane_at + column * LANES
+        for part in range(size_dp):
+            span = slice(part * group, (part + 1) * group)
+            sel[span, lanes] = jnp.where(ask_col_ref[span, :] == here, 1.0, 0.0).astype(BF16)
+        return carry
+
+    lax.fori_loop(0, columns, fill_sel, 0)
 
     def pick(table, target):
         def body(part, carry):
@@ -308,33 +338,25 @@
     pick(grad_tab, v_src)
     v_one.start()
 
-    lax.fori_loop(columns // 4, columns, fill_adj, 0)
-
+    q_one.start()
+    p_one.arrive()
+    p_two.start()
+    lax.fori_loop(0, columns // 4, fill_adj, 0)
     x_one.arrive()
     x_two.start()
+    lax.fori_loop(columns // 4, columns // 2, fill_adj, 0)
+    e_one.arrive()
+    e_two.start()
+    lax.fori_loop(columns // 2, columns, fill_adj, 0)
+    v_one.arrive()
+    v_two.start()
+    q_one.arrive()
+    q_two.start()
 
     chunks = rows // CHUNK
 
     def at_chunk(step):
         return pl.ds(pl.multiple_of(step * CHUNK, CHUNK), CHUNK)
-
-    loads["up"].wait()
-    for part in range(size_dp):
-        p_src[part] = dot(hal_t[part * group : (part + 1) * group, :], up[...]).astype(BF16)
-
-    e_one.arrive()
-    e_two.start()
-
-    def own_spread(step, carry):
-        here = at_chunk(step)
-        spread_own[here, :] = dot(adj_t[here, :], up[...])
-        return carry
-
-    lax.fori_loop(0, chunks // 2, own_spread, 0)
-    v_one.arrive()
-    v_two.start()
-    p_one.start()
-    lax.fori_loop(chunks // 2, chunks, own_spread, 0)
 
     loads["feats"].wait()
     feats_t[...] = feats[...].T
@@ -362,8 +384,12 @@
 
     lax.fori_loop(0, chunks, own_two, 0)
 
-    p_one.arrive()
-    p_two.start()
+    def own_spread(step, carry):
+        here = at_chunk(step)
+        spread_own[here, :] = dot(adj_t[here, :], up[...])
+        hal[here, :] = hal_t[:, here].T
+        return carry
+
 
     e_two.arrive()
     he_t = e_fin[...].reshape(halo, e_fin.shape[-1]).T
@@ -379,15 +405,33 @@
         strip = agg2_t[peer * part2 : (peer + 1) * part2, :]
         t2_src[peer] = dot(strip, up[...]).astype(BF16)
     t2_one.start()
-
     loads["w2"].wait()
+
+    def output(step, carry):
+        here = at_chunk(step)
+        out_buf[here, :] = dot(agg2_t[:, here], w2[...], TN).astype(BF16)
+        return carry
+
+    lax.fori_loop(0, chunks, own_spread, 0)
+    lax.fori_loop(0, chunks, output, 0)
+
+    def total(ref, count):
+        value = ref[0].astype(F32)
+        for at in range(1, count):
+            value = value + ref[at].astype(F32)
+        return value
+
+    t2_one.arrive()
+    t2_sum[...] = total(t2_mid, size_mp).astype(BF16)
+    t2_two.start()
+
     v_two.arrive()
     term1[...] = jnp.zeros_like(term1)
     hv = v_fin[...].reshape(halo, v_fin.shape[-1])
 
     def backward(step, carry):
         here = at_chunk(step)
-        spread = (spread_own[here, :] + dot(hal_t[:, here], hv, TN)).astype(BF16)
+        spread = (spread_own[here, :] + dot(hal[here, :], hv)).astype(BF16)
         back = dot(w2[...], spread, NT)
         d_pre = (back * dfac_t[:, here]).astype(BF16)
         term1[...] += dot(agg1_t[:, here], d_pre, NT)
@@ -399,47 +443,28 @@
         t1_src[peer] = term1[peer * part1 : (peer + 1) * part1, :].astype(BF16)
     t1_one.start()
 
-    def total(ref, count):
-        value = ref[0].astype(F32)
-        for at in range(1, count):
-            value = value + ref[at].astype(F32)
-        return value
-
-    t2_one.arrive()
-    t2_sum[...] = total(t2_mid, size_mp).astype(BF16)
-    t2_two.start()
-
-    def output(step, carry):
+    q_two.arrive()
+    p_two.arrive()
+    hp = p_fin[...].reshape(halo, half)
+    hq = q_fin[...].reshape(halo, half)
+
+    def owner_sum(step, carry):
         here = at_chunk(step)
-        out_buf[here, :] = dot(agg2_t[:, here], w2[...], TN).astype(BF16)
-        return carry
-
-    lax.fori_loop(0, chunks, output, 0)
-    out_store = pltpu.make_async_copy(out_buf, out_hbm, store_sem.at[0])
-    out_store.start()
-
+        hgrad_buf[here, 0:half] = dot(sel[:, here], hp, TN).astype(BF16)
+        hgrad_buf[here, half:] = dot(sel[:, here], hq, TN).astype(BF16)
+        return carry
+
+    lax.fori_loop(0, chunks // 2, owner_sum, 0)
+    t2_two.arrive()
+    t2_all[me_mp] = (total(t2_fin, size_dp) * factor).astype(BF16)
+    gather_start(t2_three)
     t1_one.arrive()
     t1_sum[...] = total(t1_mid, size_mp).astype(BF16)
     t1_two.start()
-    t2_two.arrive()
-    t2_all[me_mp] = (total(t2_fin, size_dp) * factor).astype(BF16)
-    gather_start(t2_three)
-
-    p_two.arrive()
-    hp = p_fin[...].reshape(halo, p_fin.shape[-1])
-
-    def owner_sum(step, carry):
-        here = at_chunk(step)
-        hgrad_buf[here, :] = dot(sel[:, here], hp, TN).astype(BF16)
-        return carry
-
-    lax.fori_loop(0, chunks // 2, owner_sum, 0)
+    lax.fori_loop(chunks // 2, chunks, owner_sum, 0)
     t1_two.arrive()
     t1_all[me_mp] = (total(t1_fin, size_dp) * factor).astype(BF16)
     gather_start(t1_three)
-    lax.fori_loop(chunks // 2, chunks, owner_sum, 0)
-    hgrad_store = pltpu.make_async_copy(hgrad_buf, hgrad_hbm, store_sem.at[1])
-    hgrad_store.start()
 
     gather_arrive(t2_three)
     for peer in range(size_mp):
@@ -449,8 +474,6 @@
         g1_ref[peer * part1 : (peer + 1) * part1, :] = t1_all[peer].astype(F32)
     for hop in hops:
         hop.finish()
-    out_store.wait()
-    hgrad_store.wait()
 
 
 def local_kernel(
@@ -476,18 +499,8 @@
     hid_in, hid = weight_two.shape
     per_peer = halo // (size_dp * size_mp)
     group = size_mp * per_peer
+    lines, halo_lines = rows // LANES, halo // LANES
     factor = 1.0 / float(rows * size_dp * size_mp) ** 0.5
-    tail = jnp.concatenate([halo_deg, halo_rows % shard_rows, jnp.zeros((rows - 2 * halo,), I32)])
-    packed = jnp.concatenate(
-        [
-            batch_nbrs.T,
-            halo_nbrs.T,
-            batch_deg[None],
-            halo_len[None],
-            tail[None],
-            jnp.zeros((5, rows), I32),
-        ]
-    )
     any_spec = pl.BlockSpec(memory_space=pl.ANY)
     vmem_spec = pl.BlockSpec(memory_space=pltpu.VMEM)
     vmem = pltpu.VMEM
@@ -508,15 +521,20 @@
     return pl.pallas_call(
         functools.partial(kernel, size_dp, size_mp, per_peer, factor),
         out_shape=(
-            jax.ShapeDtypeStruct((rows, hid), BF16),
-            jax.ShapeDtypeStruct((shard_rows, hid), BF16),
-            jax.ShapeDtypeStruct((feat, hid), F32),
-            jax.ShapeDtypeStruct((hid_in, hid), F32),
+            pltpu.VMEM((rows, hid), BF16),
+            pltpu.VMEM((shard_rows, hid), BF16),
+            pltpu.VMEM((feat, hid), F32),
+            pltpu.VMEM((hid_in, hid), F32),
         ),
-        in_specs=[any_spec] * 8,
-        out_specs=(any_spec, any_spec, vmem_spec, vmem_spec),
+        in_specs=[any_spec] * 13,
+        out_specs=(vmem_spec,) * 4,
         scratch_shapes=[
-            vmem(packed.shape, I32),
+            vmem((batch_nbrs.shape[1], rows), I32),
+            vmem((halo_nbrs.shape[1], rows), I32),
+            vmem((lines, LANES), I32),
+            vmem((lines, LANES), I32),
+            vmem((halo_lines, LANES), I32),
+            vmem((halo_lines, LANES), I32),
             vmem(node_feats.shape, BF16),
             vmem(feat_table.shape, BF16),
             vmem(emb_table.shape, BF16),
@@ -528,6 +546,7 @@
             vmem((size_mp, size_dp * 8, group), I32),
             vmem((size_dp, 8, group), I32),
             vmem((size_dp, 8, group), I32),
+            vmem((halo, LANES), I32),
             vmem((rows, LANES), F32),
             vmem((halo, LANES), F32),
             vmem((rows, rows), BF16),
@@ -536,7 +555,8 @@
             *three(feat),
             *three(hid),
             *three(hid),
-            *three(hid),
+            *three(hid // 2),
+            *three(hid // 2),
             vmem((feat, rows), BF16),
             vmem((feat, rows), BF16),
             vmem((hid, rows), BF16),
@@ -545,23 +565,27 @@
             vmem((hid, rows), BF16),
             vmem((rows, hid), F32),
             vmem((feat, hid), F32),
-            vmem((8, LANES), F32),
-            vmem((rows, hid), BF16),
-            vmem((shard_rows, hid), BF16),
+            vmem((rows, halo), BF16),
             *sums(part1),
             *sums(part2),
-            pltpu.SemaphoreType.DMA((8,)),
-            pltpu.SemaphoreType.DMA((2,)),
-            pltpu.SemaphoreType.DMA((16,)),
-            pltpu.SemaphoreType.DMA((9, size_mp)),
-            pltpu.SemaphoreType.DMA((9, size_mp)),
-            pltpu.SemaphoreType.DMA((7, size_dp)),
-            pltpu.SemaphoreType.DMA((7, size_dp)),
+            pltpu.SemaphoreType.DMA((13,)),
+            pltpu.SemaphoreType.DMA((18,)),
+            pltpu.SemaphoreType.DMA((10, size_mp)),
+            pltpu.SemaphoreType.DMA((10, size_mp)),
+            pltpu.SemaphoreType.DMA((8, size_dp)),
+            pltpu.SemaphoreType.DMA((8, size_dp)),
         ],
         compiler_params=pltpu.CompilerParams(
-            collective_id=0, has_side_effects=True, vmem_limit_bytes=60 * 1024 * 1024
+            collective_id=0, has_side_effects=True, vmem_limit_bytes=VMEM_MIB * 1024 * 1024
         ),
-    )(packed, node_feats, feat_table, emb_table, grad_table, weight_one, weight_two, grad_out)
+    )(
+        batch_nbrs.T,
+        halo_nbrs.T,
+        batch_deg.reshape(lines, LANES),
+        halo_len.reshape(lines, LANES),
+        halo_deg.reshape(halo_lines, LANES),
+        halo_rows.reshape(halo_lines, LANES),
+        node_feats, feat_table, emb_table, grad_table, weight_one, weight_two, grad_out)
 
 
 def matrices(batch_deg, batch_nbrs, halo_nbrs, halo_len, halo_deg):

time: 91.7 us -> 88.2 us (0.962)
  local copies, waits for them, and re-layouts: 10.6 us -> 4.31 us
  Pallas kernels: 78.7 us -> 83.1 us
  other arithmetic: 1.38 us -> 0 us
    pallas_call x1, Pallas kernels: 78.7 us -> 83.1 us  [local_kernel(): pl.pallas_call(functools.partial(kernel, size_dp, size_mp, per_peer, fact...]
    concatenate x1 -> x0, local copies, waits for them, and re-layouts: 4.33 us -> none  [local_kernel(): jnp.concatenate([batch_nbrs.T, halo_nbrs.T, batch_deg[None], halo_len[Non...]
    unnamed x10 -> x4, local copies, waits for them, and re-layouts: 6.23 us -> 4.31 us
where the time goes in v1:
time: 88.2 us; the launch traced here: 88.1 us
  Pallas kernels  83.1 us (94%)
  local copies, waits for them, and re-layouts  4.31 us (5%)
    pallas_call x1, Pallas kernels, local_kernel(): pl.pallas_call(functools.partial(kernel, size_dp, size_mp, per_peer, fact...  83.1 us
    unnamed x4, local copies, waits for them, and re-layouts  4.31 us

profile of v1, /device:TPU:0, one launch (start us, length us, event | category | flops | bytes accessed | tf_op | source)
XLA Modules:
  0.0 88.1 jit_solution(16460786574203101843)
XLA Ops:
  0.6 83.1 %shard_map.156 = (bf16[2048,512]{1,0:T(8,128)(2,1)S(1)}, bf16[2048,512]{1,0:T(8,128)(2,1)S(1)}, f32[128,512]{1,0:T(8,128)S(1)}, f32[512,512]{1,0:T(8,128)S(1)}) custom-call(s32[8,2048]{1,0:T(8,128)} %bitcast.6, s32[8,2048]{1,0:T(8,128)} %bitcast.7, s32[16,128]{1,0:T(8,128)} %bitcast.8, s32[16,128]{1,0:T(8,128)} %bitcast.9, s32[4,128]{1,0:T(4,128)} %bitcast.10, ...), custom_call_target="tpu_custom_call" | custom-call | tf_op jit(solution)/shard_map/pallas_call | solution.py:521
  83.8 1.3 %copy.21 = bf16[2048,512]{1,0:T(8,128)(2,1)} copy(bf16[2048,512]{1,0:T(8,128)(2,1)S(1)} %get-tuple-element.4) | data formatting | bytes 4194304
  85.1 0.7 copy.23
  85.8 1.0 %copy.24 = f32[512,512]{1,0:T(8,128)} copy(f32[512,512]{1,0:T(8,128)S(1)} %get-tuple-element.7) | data formatting | bytes 2097152
  86.7 1.3 %copy.22 = bf16[2048,512]{1,0:T(8,128)(2,1)} copy(bf16[2048,512]{1,0:T(8,128)(2,1)S(1)} %get-tuple-element.5) | data formatting | bytes 4194304

commit v2 on v1

--- a/solution.py
+++ b/solution.py
@@ -11,7 +11,7 @@
 BF16 = jnp.bfloat16
 I32 = jnp.int32
 LANES = 128
-CHUNK = 256
+CHUNK = 512
 VMEM_MIB = 54
 NN = (((1,), (0,)), ((), ()))
 NT = (((1,), (1,)), ((), ()))
@@ -296,10 +296,9 @@
 
     loads["up"].wait()
     half = p_src.shape[2]
-    for part in range(size_dp):
-        message = dot(hal_t[part * group : (part + 1) * group, :], up[...]).astype(BF16)
-        p_src[part] = message[:, 0:half]
-        q_src[part] = message[:, half:]
+    message = dot(hal_t[...], up[...]).astype(BF16)
+    p_src[...] = message[:, 0:half].reshape(p_src.shape)
+    q_src[...] = message[:, half:].reshape(q_src.shape)
     p_one.start()
     loads["nbrs"].wait()
     spread_out(inv_col, deg)
@@ -321,12 +320,7 @@
     lax.fori_loop(0, columns, fill_sel, 0)
 
     def pick(table, target):
-        def body(part, carry):
-            here = pl.ds(pl.multiple_of(part * group, group), group)
-            target[part] = dot(sel[here, :], table[...]).astype(BF16)
-            return carry
-
-        lax.fori_loop(0, size_dp, body, 0)
+        target[...] = dot(sel[...], table[...]).astype(BF16).reshape(target.shape)
 
     loads["feat"].wait()
     pick(feat_tab, x_src)
@@ -385,7 +379,7 @@
     lax.fori_loop(0, chunks, own_two, 0)
 
     def own_spread(step, carry):
-        here = at_chunk(step)
+        here = pl.ds(pl.multiple_of(step * 2 * CHUNK, 2 * CHUNK), 2 * CHUNK)
         spread_own[here, :] = dot(adj_t[here, :], up[...])
         hal[here, :] = hal_t[:, here].T
         return carry
@@ -401,9 +395,7 @@
 
     lax.fori_loop(0, chunks, layer_two, 0)
     part2 = t2_src.shape[1]
-    for peer in range(size_mp):
-        strip = agg2_t[peer * part2 : (peer + 1) * part2, :]
-        t2_src[peer] = dot(strip, up[...]).astype(BF16)
+    t2_src[...] = dot(agg2_t[...], up[...]).astype(BF16).reshape(t2_src.shape)
     t2_one.start()
     loads["w2"].wait()
 
@@ -412,7 +404,7 @@
         out_buf[here, :] = dot(agg2_t[:, here], w2[...], TN).astype(BF16)
         return carry
 
-    lax.fori_loop(0, chunks, own_spread, 0)
+    lax.fori_loop(0, chunks // 2, own_spread, 0)
     lax.fori_loop(0, chunks, output, 0)
 
     def total(ref, count):
@@ -445,13 +437,13 @@
 
     q_two.arrive()
     p_two.arrive()
-    hp = p_fin[...].reshape(halo, half)
-    hq = q_fin[...].reshape(halo, half)
+    arrived = jnp.concatenate(
+        [p_fin[...].reshape(halo, half), q_fin[...].reshape(halo, half)], axis=1
+    )
 
     def owner_sum(step, carry):
         here = at_chunk(step)
-        hgrad_buf[here, 0:half] = dot(sel[:, here], hp, TN).astype(BF16)
-        hgrad_buf[here, half:] = dot(sel[:, here], hq, TN).astype(BF16)
+        hgrad_buf[here, :] = dot(sel[:, here], arrived, TN).astype(BF16)
         return carry
 
     lax.fori_loop(0, chunks // 2, owner_sum, 0)

time: 88.2 us -> 80.1 us (0.908)
  Pallas kernels: 83.1 us -> 75 us
    pallas_call x1, Pallas kernels: 83.1 us -> 75 us  [local_kernel(): pl.pallas_call(functools.partial(kernel, size_dp, size_mp, per_peer, fact...]
where the time goes in v2:
time: 80.1 us; the launch traced here: 80 us
  Pallas kernels  75 us (94%)
  local copies, waits for them, and re-layouts  4.31 us (5%)
    pallas_call x1, Pallas kernels, local_kernel(): pl.pallas_call(functools.partial(kernel, size_dp, size_mp, per_peer, fact...  75 us
    unnamed x4, local copies, waits for them, and re-layouts  4.31 us

profile of v2, /device:TPU:0, one launch (start us, length us, event | category | flops | bytes accessed | tf_op | source)
XLA Modules:
  0.0 80.0 jit_solution(12618928073489933676)
XLA Ops:
  0.6 75.0 %shard_map.156 = (bf16[2048,512]{1,0:T(8,128)(2,1)S(1)}, bf16[2048,512]{1,0:T(8,128)(2,1)S(1)}, f32[128,512]{1,0:T(8,128)S(1)}, f32[512,512]{1,0:T(8,128)S(1)}) custom-call(s32[8,2048]{1,0:T(8,128)} %bitcast.6, s32[8,2048]{1,0:T(8,128)} %bitcast.7, s32[16,128]{1,0:T(8,128)} %bitcast.8, s32[16,128]{1,0:T(8,128)} %bitcast.9, s32[4,128]{1,0:T(4,128)} %bitcast.10, ...), custom_call_target="tpu_custom_call" | custom-call | tf_op jit(solution)/shard_map/pallas_call | solution.py:513
  75.6 1.3 %copy.21 = bf16[2048,512]{1,0:T(8,128)(2,1)} copy(bf16[2048,512]{1,0:T(8,128)(2,1)S(1)} %get-tuple-element.4) | data formatting | bytes 4194304
  77.0 0.7 copy.23
  77.7 1.0 %copy.24 = f32[512,512]{1,0:T(8,128)} copy(f32[512,512]{1,0:T(8,128)S(1)} %get-tuple-element.7) | data formatting | bytes 2097152
  78.6 1.3 %copy.22 = bf16[2048,512]{1,0:T(8,128)(2,1)} copy(bf16[2048,512]{1,0:T(8,128)(2,1)S(1)} %get-tuple-element.5) | data formatting | bytes 4194304
